TPU v7x, 256 devices: a whole 4x4x8 slice. The times are simulated.
256 devices in a mesh: section: 2 (over z_hi), dp: 8 (over y, core), mp: 16 (over z_lo, x).
Axes of the slice: x: 4, y: 4, z: 8 (z_hi: 2, z_lo: 4; z = z_hi * 4 + z_lo), core: 2. Of those that a mesh axis runs over, the one named last changes fastest.
Arguments:
- loss_sensitivity_outgoing: bfloat16 [2, 1536, 8192], P('section', ('dp', 'mp')), may hold values from -6 to 6
- expansion_factor: bfloat16 [2, 8192, 32768], P('section', 'dp', 'mp'), may hold values from -0.0508233 to 0.0508233
- contraction_factor: bfloat16 [2, 32768, 8192], P('section', 'mp', 'dp'), may hold values from -0.03125 to 0.03125
- intermediate_affine_values: bfloat16 [2, 1536, 32768], P('section', 'dp', 'mp'), may hold values from -6 to 6
- centered_unscaled_entry: bfloat16 [2, 1536, 8192], P('section', 'mp', 'dp'), may hold values from -4.5 to 4.5
- inverse_spread_per_position: float32 [2, 1536], P('section', 'mp'), may hold values from 0.3 to 3
- layernorm_multiplier: float32 [2, 8192], P('section', 'dp'), may hold values from 0.25 to 3
Outputs:
- grad_out: bfloat16 [2, 1536, 8192], P('section', 'mp', 'dp')
All inputs are finite; a program needn't handle non-finite values.
Results may differ from a plain program's by a relative error of at most 0.02.
Values may be sent and summed in bfloat16 or wider, within the bound.
No kernel may reach another device: no remote copies, remote signals or barrier semaphores. Data moves between devices by JAX's collectives and lax.ppermute only.
A program may use at most 64 MiB of HBM per device.

v0:
```python
import math

import jax
import jax.numpy as jnp
from jax import lax
from jax.sharding import PartitionSpec as P

D = 8192


def from_partner(array, axis, apart):
    return lax.ppermute(array, axis, [(i, i ^ 1 << apart) for i in range(lax.axis_size(axis))])


def gelu_slope(u):
    c = math.sqrt(2.0 / math.pi)
    t = jnp.tanh(c * (u + 0.044715 * u * u * u))
    return 0.5 * (1.0 + t) + 0.5 * u * (1.0 - t * t) * c * (1.0 + 3.0 * 0.044715 * u * u)


def contract_rows(rows, weight_matrix):
    return lax.dot_general(
        rows, weight_matrix, (((1,), (1,)), ((), ())), preferred_element_type=jnp.float32
    )


def per_device(
    loss_sensitivity_outgoing,
    expansion_factor,
    contraction_factor,
    intermediate_affine_values,
    centered_unscaled_entry,
    inverse_spread_per_position,
    layernorm_multiplier,
):
    incoming = from_partner(loss_sensitivity_outgoing[0], "section", 0)
    n_data = lax.axis_size("dp")
    n_model = lax.axis_size("mp")
    spread = lax.all_to_all(incoming, "dp", split_axis=1, concat_axis=0, tiled=True)
    feat_width = spread.shape[1]
    stacked = spread.reshape(n_data, 1, incoming.shape[0], feat_width)
    full_rows = lax.all_gather(stacked, "mp", axis=1, tiled=True)
    upstream = full_rows.reshape(-1, feat_width)
    up_block = expansion_factor[0]
    down_block = contraction_factor[0]
    grad_hidden = lax.psum_scatter(
        contract_rows(upstream, down_block).astype(jnp.bfloat16),
        "dp",
        scatter_dimension=0,
        tiled=True,
    ).astype(jnp.float32)
    slope = (grad_hidden * gelu_slope(intermediate_affine_values[0].astype(jnp.float32))).astype(
        jnp.bfloat16
    )
    mine = upstream.shape[0] // n_model
    offset = lax.axis_index("mp") * mine
    partial_value = contract_rows(lax.all_gather(slope, "dp", axis=0, tiled=True), up_block)
    summed = lax.psum(partial_value.astype(jnp.bfloat16), "mp").astype(jnp.float32)
    grad_norm = lax.dynamic_slice_in_dim(summed, offset, mine, 0)
    own_upstream = lax.dynamic_slice_in_dim(upstream, offset, mine, 0).astype(jnp.float32)
    scaled = layernorm_multiplier[0][None, :] * grad_norm
    standardized_entry = centered_unscaled_entry[0].astype(jnp.float32)
    first, second = lax.psum(
        (jnp.sum(scaled, axis=1), jnp.sum(scaled * standardized_entry, axis=1)), "dp"
    )
    result = own_upstream + inverse_spread_per_position[0][:, None] * (
        scaled - first[:, None] / D - standardized_entry * second[:, None] / D
    )
    return result.astype(jnp.bfloat16)[None]


def solution(mesh):
    in_specs = (
        P("section", ("dp", "mp"), None),
        P("section", "dp", "mp"),
        P("section", "mp", "dp"),
        P("section", "dp", "mp"),
        P("section", "mp", "dp"),
        P("section", "mp"),
        P("section", "dp"),
    )
    out_specs = P("section", "mp", "dp")
    return jax.shard_map(
        per_device, mesh=mesh, in_specs=in_specs, out_specs=out_specs, check_vma=False
    )
```

profile of v0, /device:TPU:1, one launch (start us, length us, event | category | flops | bytes accessed | tf_op | source)
XLA Modules:
  0.0 434.6 jit_solution(15221356500011211660)
XLA Ops:
  6.5 7.7 %collective-permute-start = (bf16[12,8192]{1,0:T(8,128)(2,1)}, bf16[12,8192]{1,0:T(8,128)(2,1)S(1)}, u32[]{:S(2)}, u32[]{:S(2)}) collective-permute-start(bf16[12,8192]{1,0:T(8,128)(2,1)} %bitcast.35), channel_id=1, source_target_pairs={{0,128},{128,0},{1,129},{129,1},{2,130},{130,2},{3,131},{131,3},{4... | collective-permute-start | bytes 589832 | tf_op jit(solution)/shard_map/ppermute | solution.py:12
  14.3 5.7 %collective-permute-done = bf16[12,8192]{1,0:T(8,128)(2,1)S(1)} collective-permute-done((bf16[12,8192]{1,0:T(8,128)(2,1)}, bf16[12,8192]{1,0:T(8,128)(2,1)S(1)}, u32[]{:S(2)}, u32[]{:S(2)}) %collective-permute-start) | collective-permute-done | bytes 196640 | tf_op jit(solution)/shard_map/ppermute | solution.py:12
  20.0 0.1 copy.15
  20.2 0.1 copy.12
  20.3 13.7 %all_to_all.16 = bf16[12,8,1024]{2,0,1:T(8,128)(2,1)S(1)} all-to-all(bf16[12,8,1024]{2,0,1:T(8,128)(2,1)S(1)} %copy.12), channel_id=1, replica_groups=mesh['section'=2,'dp'=8,'mp'=16] {'dp'}, dimensions={1} | all-to-all | bytes 393216 | tf_op jit(solution)/shard_map/all_to_all | solution.py:39
  33.9 0.8 copy.13
  34.7 0.0 all-gather.6.cloned.1.call-update
  34.8 0.0 reduce-scatter.2.cloned.1.call-start
  34.8 80.3 %all-gather.6.cloned.1.call-done = bf16[8,192,1024]{2,0,1:T(8,128)(2,1)} async-done(((bf16[8,12,1024]{2,0,1:T(8,128)(2,1)}), bf16[8,192,1024]{2,0,1:T(8,128)(2,1)}) %all-gather.6.cloned.1.call-update) | async-done | bytes 3145744 | tf_op jit(solution)/shard_map/all_gather | solution.py:42
  115.2 3.8 copy.14
  118.9 8.7 %convolution_convert_fusion = bf16[1536,2048]{1,0:T(8,128)(2,1)} fusion(bf16[1536,1024]{1,0:T(8,128)(2,1)S(1)} %bitcast.27, bf16[1,2048,1024]{2,1,0:T(8,128)(2,1)S(1)} %copy-done.3), kind=kOutput, calls=%fused_computation | convolution fusion | flops 6445596672 | bytes 13631488 | tf_op jit(solution)/shard_map/dot_general | solution.py:22
  127.6 0.0 reduce-scatter.2.cloned.1.call-update
  127.7 0.0 all-gather.4.cloned.1.call-start
  127.7 52.4 %reduce-scatter.2.cloned.1.call-done = bf16[192,2048]{1,0:T(8,128)(2,1)} async-done(((bf16[1536,2048]{1,0:T(8,128)(2,1)}), bf16[192,2048]{1,0:T(8,128)(2,1)}) %reduce-scatter.2.cloned.1.call-update) | async-done | bytes 786448 | tf_op jit(solution)/shard_map/reduce_scatter | solution.py:46
  180.1 3.3 fusion.13
  183.4 0.0 all-gather.4.cloned.1.call-update
  183.5 0.0 all-reduce.3.cloned.1.call-start
  183.5 44.3 %all-gather.4.cloned.1.call-done = bf16[1536,2048]{1,0:T(8,128)(2,1)} async-done(((bf16[192,2048]{1,0:T(8,128)(2,1)}), bf16[1536,2048]{1,0:T(8,128)(2,1)}) %all-gather.4.cloned.1.call-update) | async-done | bytes 6291472 | tf_op jit(solution)/shard_map/all_gather | solution.py:57
  227.8 11.3 %fusion.3 = bf16[1536,1024]{1,0:T(8,128)(2,1)} fusion(bf16[1536,2048]{1,0:T(8,128)(2,1)} %all-gather.4.cloned.1.call-done, bf16[1,1024,2048]{2,1,0:T(8,128)(2,1)} %param.8), kind=kOutput, calls=%fused_computation.11 | convolution fusion | flops 6444023808 | bytes 13631488 | tf_op jit(solution)/shard_map/dot_general | solution.py:22
  239.1 0.0 all-reduce.3.cloned.1.call-update
  239.1 163.7 %all-reduce.3.cloned.1.call-done = bf16[1536,1024]{1,0:T(8,128)(2,1)} async-done(((bf16[1536,1024]{1,0:T(8,128)(2,1)}), bf16[1536,1024]{1,0:T(8,128)(2,1)}) %all-reduce.3.cloned.1.call-update) | async-done | bytes 3145744 | tf_op jit(solution)/shard_map/psum | solution.py:58
  402.9 1.1 fusion.21
  404.0 22.2 %all-reduce = (f32[96]{0:T(128)S(1)}, f32[96]{0:T(128)S(1)}) all-reduce(f32[96]{0:T(128)S(1)} %get-tuple-element.6, f32[96]{0:T(128)S(1)} %get-tuple-element.5), channel_id=1, replica_groups=mesh['section'=2,'dp'=8,'mp'=16] {'dp'}, use_global_device_ids=true, to_apply=%region_5.0 | all-reduce | flops 192 | bytes 1536 | tf_op jit(solution)/shard_map/psum | solution.py:63
  426.2 1.8 fusion.22
  (11 shorter events, 0.0 us)
Async XLA Ops:
  6.5 108.6 %all-gather.6.cloned.1.call-start = ((), (), s32[]{:S(2)}) async-start(), calls=%async_computation.5 | async-start | bytes 3342336 | tf_op jit(solution)/shard_map/all_gather | solution.py:42
  6.5 13.4 %collective-permute-start = (bf16[12,8192]{1,0:T(8,128)(2,1)}, bf16[12,8192]{1,0:T(8,128)(2,1)S(1)}, u32[]{:S(2)}, u32[]{:S(2)}) collective-permute-start(bf16[12,8192]{1,0:T(8,128)(2,1)} %bitcast.35), channel_id=1, source_target_pairs={{0,128},{128,0},{1,129},{129,1},{2,130},{130,2},{3,131},{131,3},{4... | collective-permute-start | bytes 589832 | tf_op jit(solution)/shard_map/ppermute | solution.py:12
  34.8 145.3 %reduce-scatter.2.cloned.1.call-start = ((), (), s32[]{:S(2)}) async-start(), calls=%async_computation.2 | async-start | bytes 7077888 | tf_op jit(solution)/shard_map/reduce_scatter | solution.py:46
  115.2 3.8 copy-start.3
  127.7 100.2 %all-gather.4.cloned.1.call-start = ((), (), s32[]{:S(2)}) async-start(), calls=%async_computation.3 | async-start | bytes 7077888 | tf_op jit(solution)/shard_map/all_gather | solution.py:57
  183.5 219.4 %all-reduce.3.cloned.1.call-start = ((), (), s32[]{:S(2)}) async-start(), calls=%async_computation.4 | async-start | bytes 6291456 | tf_op jit(solution)/shard_map/psum | solution.py:58
  239.1 163.8 %copy-start = (bf16[1,96,1024]{2,1,0:T(8,128)(2,1)S(1)}, bf16[1,96,1024]{2,1,0:T(8,128)(2,1)}, u32[]{:S(2)}) copy-start(bf16[1,96,1024]{2,1,0:T(8,128)(2,1)} %param.11) | copy-start | bytes 589828
  239.1 163.8 %copy-start.1 = (f32[1,1024]{1,0:T(1,128)S(1)}, f32[1,1024]{1,0:T(1,128)}, u32[]{:S(2)}) copy-start(f32[1,1024]{1,0:T(1,128)} %param.13) | copy-start | bytes 12292
  239.1 187.1 %copy-start.2 = (f32[1,96]{1,0:T(1,128)S(1)}, f32[1,96]{1,0:T(1,128)}, u32[]{:S(2)}) copy-start(f32[1,96]{1,0:T(1,128)} %param.12) | copy-start | bytes 1156
Sparse Core Ops, SparseCore 0:
  34.9 80.2 all-gather.5
  127.8 52.2 reduce-scatter.1
  183.6 44.2 all-gather.3
  239.3 163.5 all-reduce.2
where the time goes:
time: 435 us
  waiting for transfers between devices  347 us (80%)
  blocking collectives  35.9 us (8%)
  matrix products  20 us (5%)
  between operations  13.2 us (3%)
  starting transfers between devices  7.87 us (2%)
  other arithmetic  6.29 us (1%)
  local copies, waits for them, and re-layouts  4.85 us (1%)
    psum x1, waiting for transfers between devices, per_device(): lax.psum(partial_value.astype(jnp.bfloat16), 'mp').astype(jnp.float32)  164 us
    all_gather x1, waiting for transfers between devices, per_device(): full_rows = lax.all_gather(stacked, 'mp', axis=1, tiled=True)  80.3 us
    reduce_scatter x1, waiting for transfers between devices, per_device(): lax.psum_scatter(contract_rows(upstream, down_block).astype(jnp.bfloat16)...  52.4 us
    all_gather x1, waiting for transfers between devices, per_device(): lax.all_gather(slope, 'dp', axis=0, tiled=True)  44.3 us
    psum x1, blocking collectives, per_device(): lax.psum((jnp.sum(scaled, axis=1), jnp.sum(scaled * standardized_entry, a...  22.2 us
    dot_general x2, matrix products, contract_rows(): lax.dot_general(rows, weight_matrix, (((1,), (1,)), ((), ())), preferred_...  20 us
    all_to_all x1, blocking collectives, per_device(): lax.all_to_all(incoming, 'dp', split_axis=1, concat_axis=0, tiled=True)  13.7 us
  transfers between devices with their start and end apart: 5, of which 5 were waited for; matrix products, arithmetic and copies ran while one was open for 0% of the time, Pallas kernels for 0%

commit v1 on v0

v1 whole, which is shorter than its diff:
```python
import functools
import math

import jax
import jax.numpy as jnp
from jax import lax
from jax.experimental import pallas as pl
from jax.experimental.pallas import tpu as pltpu
from jax.sharding import Mesh, PartitionSpec as P

BF = jnp.bfloat16
F32 = jnp.float32
CHUNKS = 3


def move_z(array, flip):
    return lax.ppermute(array, "z", [(z, z ^ flip) for z in range(4)])


def move_section(array, flip):
    pairs = [(4 * s + z, 4 * (1 - s) + (z ^ flip)) for s in range(2) for z in range(4)]
    return lax.ppermute(array, ("section", "z"), pairs)


def move_core(array):
    return lax.ppermute(array, "core", [(0, 1), (1, 0)])


def gelu_slope(u):
    c = math.sqrt(2.0 / math.pi)
    t = jnp.tanh(c * (u + 0.044715 * u * u * u))
    return 0.5 * (1.0 + t) + 0.5 * u * (1.0 - t * t) * c * (1.0 + 3.0 * 0.044715 * u * u)


def nt_dot(left, right):
    return lax.dot_general(left, right, (((1,), (1,)), ((), ())), preferred_element_type=F32)


def full(shape):
    return pl.BlockSpec(shape, lambda i: (0,) * len(shape))


def hidden_kernel(pos, gathered, weight, send, keep, mine, lhs):
    x, y, z, c = pos[0], pos[1], pos[2], pos[3]

    @pl.when(pl.program_id(0) == 0)
    def _():
        for c_rel in range(2):
            for y_at in range(4):
                source = 2 * y_at + jnp.bitwise_xor(c, c_rel)
                for x_at in range(4):
                    lhs[4 * c_rel + y_at, x_at] = gathered[x_at, source]
        rows = lhs[4 * jnp.bitwise_xor(c, x // 2) + z].astype(F32).reshape(4, 2, 8, -1)
        picked = jnp.where(lax.rem(x, 2) == 0, rows[:, 0], rows[:, 1])
        mine[...] = picked.reshape(32, -1).astype(BF)

    rows = lhs[...].reshape(512, -1)
    product = nt_dot(rows, weight[...]).astype(BF)
    keep[...] = product[:256].reshape(keep.shape)
    send[...] = product[256:].reshape(send.shape)


def hidden_product(pos, gathered, weight):
    width = weight.shape[0]
    depth = weight.shape[1]
    tile = min(512, width)
    out_block = pl.BlockSpec((4, 64, tile), lambda i: (0, 0, i))
    return pl.pallas_call(
        hidden_kernel,
        grid=(width // tile,),
        in_specs=[
            pl.BlockSpec(memory_space=pltpu.SMEM),
            full(gathered.shape),
            pl.BlockSpec((tile, depth), lambda i: (i, 0)),
        ],
        out_specs=[out_block, out_block, full((32, depth))],
        out_shape=[
            jax.ShapeDtypeStruct((4, 64, width), BF),
            jax.ShapeDtypeStruct((4, 64, width), BF),
            jax.ShapeDtypeStruct((32, depth), BF),
        ],
        scratch_shapes=[pltpu.VMEM((8, 4, 16, depth), BF)],
        compiler_params=pltpu.CompilerParams(vmem_limit_bytes=40 * 2**20),
        cost_estimate=pl.CostEstimate(
            flops=2 * 512 * width * depth, bytes_accessed=2 * (width * depth + 512 * (width + depth)), transcendentals=0
        ),
    )(pos, gathered, weight)


def feature_kernel(pos, same, other, weight, out, lhs, result):
    c = pos[3]

    @pl.when(pl.program_id(0) == 0)
    def _():
        for y_at in range(4):
            lhs[2 * y_at + c] = same[y_at]
            lhs[2 * y_at + 1 - c] = other[y_at]

    rows = lhs[...].reshape(512, -1)
    result[...] = nt_dot(rows, weight[...]).reshape(result.shape)
    for x_at in range(4):
        for z_at in range(4):
            rows = result[2 * z_at + x_at // 2, :, x_at % 2]
            out[x_at, z_at] = rows.reshape(32, -1).astype(BF)


def feature_product(pos, same, other, weight):
    width = weight.shape[0]
    depth = weight.shape[1]
    tile = min(256, width)
    return pl.pallas_call(
        feature_kernel,
        grid=(width // tile,),
        in_specs=[
            pl.BlockSpec(memory_space=pltpu.SMEM),
            full(same.shape),
            full(other.shape),
            pl.BlockSpec((tile, depth), lambda i: (i, 0)),
        ],
        out_specs=pl.BlockSpec((4, 4, 32, tile), lambda i: (0, 0, 0, i)),
        out_shape=jax.ShapeDtypeStruct((4, 4, 32, width), BF),
        scratch_shapes=[pltpu.VMEM((8, 64, depth), BF), pltpu.VMEM((8, 4, 2, 8, tile), F32)],
        compiler_params=pltpu.CompilerParams(vmem_limit_bytes=40 * 2**20),
        cost_estimate=pl.CostEstimate(
            flops=2 * 512 * width * depth, bytes_accessed=2 * (width * depth + 512 * (width + depth)), transcendentals=0
        ),
    )(pos, same, other, weight)


def add(*terms):
    return functools.reduce(jnp.add, [term.astype(F32) for term in terms])


def gather_rows(part, z):
    arrived = [move_section(part, flip) for flip in range(4)]
    odd, high = z % 2 == 1, z >= 2
    a0, a1, a2, a3 = arrived
    a0, a1 = jnp.where(odd, a1, a0), jnp.where(odd, a0, a1)
    a2, a3 = jnp.where(odd, a3, a2), jnp.where(odd, a2, a3)
    a0, a2 = jnp.where(high, a2, a0), jnp.where(high, a0, a2)
    a1, a3 = jnp.where(high, a3, a1), jnp.where(high, a1, a3)
    depth = part.shape[-1]
    own = jnp.stack([a0, a1, a2, a3]).reshape(2, 2, 4, 8, depth).transpose(3, 0, 2, 1, 4).reshape(8, 16, depth)
    return lax.all_gather(own, "x", axis=0)


def reduce_hidden(send, keep):
    total = add(keep, move_core(send)).astype(BF)
    return lax.psum_scatter(total, "y", scatter_dimension=0).astype(F32)


def reduce_features(parts, z):
    total = lax.psum_scatter(parts, "x", scatter_dimension=0)

    def block(index):
        return lax.dynamic_index_in_dim(total, index, 0, keepdims=False)

    terms = [move_z(block(z ^ flip), flip) for flip in (1, 2, 3)]
    return add(block(z), *terms)


def per_device(
    loss_sensitivity_outgoing,
    expansion_factor,
    contraction_factor,
    intermediate_affine_values,
    centered_unscaled_entry,
    inverse_spread_per_position,
    layernorm_multiplier,
):
    x, y, z, c = (lax.axis_index(name) for name in ("x", "y", "z", "core"))
    pos = jnp.stack([x, y, z, c]).astype(jnp.int32)
    model = 8 * expansion_factor.shape[1]
    rows = lax.all_to_all(loss_sensitivity_outgoing[0], ("y", "core"), split_axis=1, concat_axis=0, tiled=True)
    rows = rows.reshape(8, 12, -1).transpose(1, 0, 2)

    hidden = intermediate_affine_values.shape[-1]
    slope = intermediate_affine_values[0].reshape(2, 2, 4, CHUNKS, 4, hidden)
    slope = gelu_slope(slope.transpose(3, 2, 0, 4, 1, 5).reshape(CHUNKS, 64, hidden).astype(F32))

    def by_chunk(array):
        rest = array.shape[1:]
        array = array.reshape(2, 4, CHUNKS, 4, *rest)
        array = array.transpose(2, 1, 3, 0, *range(4, array.ndim))
        return array.reshape(CHUNKS, 32, *rest)

    entry = by_chunk(centered_unscaled_entry[0]).astype(F32)
    spread = by_chunk(inverse_spread_per_position[0])
    gain = layernorm_multiplier[0]

    mine, scaled = [], []
    for k in range(CHUNKS):
        gathered = gather_rows(rows[4 * k : 4 * k + 4], z)
        send, keep, own_rows = hidden_product(pos, gathered, contraction_factor[0])
        block = (reduce_hidden(send, keep) * slope[k]).astype(BF)
        same = lax.all_gather(block, "y", axis=0)
        parts = feature_product(pos, same, move_core(same), expansion_factor[0])
        mine.append(own_rows)
        scaled.append(gain * reduce_features(parts, z))
    scaled = jnp.stack(scaled)
    upstream = jnp.stack(mine).astype(F32)
    sums = lax.psum(jnp.stack([jnp.sum(scaled, axis=2), jnp.sum(scaled * entry, axis=2)]), ("y", "core"))
    result = upstream + spread[:, :, None] * (
        scaled - sums[0][:, :, None] / model - entry * sums[1][:, :, None] / model
    )
    result = result.reshape(CHUNKS, 4, 4, 2, -1).transpose(3, 1, 0, 2, 4)
    return result.reshape(1, 96, -1).astype(BF)


def solution(mesh):
    split = Mesh(mesh.devices.reshape(2, 4, 2, 4, 4), ("section", "y", "core", "z", "x"))
    dp, mp = ("y", "core"), ("z", "x")
    in_specs = (
        P("section", dp + mp, None),
        P("section", dp, mp),
        P("section", mp, dp),
        P("section", dp, mp),
        P("section", mp, dp),
        P("section", mp),
        P("section", dp),
    )
    out_specs = P("section", mp, dp)
    return jax.shard_map(per_device, mesh=split, in_specs=in_specs, out_specs=out_specs, check_vma=False)
```

time: 435 us -> 415 us (0.954)
  waiting for transfers between devices: 347 us -> 251 us
  starting transfers between devices: 7.87 us -> 54.5 us
  local copies, waits for them, and re-layouts: 4.85 us -> 32.4 us
  Pallas kernels: 0 us -> 24.7 us
  matrix products: 20 us -> 0 us
  blocking collectives: 35.9 us -> 27.4 us
    psum x1 -> x0, waiting for transfers between devices: 164 us -> none  [per_device(): lax.psum(partial_value.astype(jnp.bfloat16), 'mp').astype(jnp.float32)]
    reduce_scatter x1 -> x6, waiting for transfers between devices: 52.4 us -> 132 us  [the longest x3 68.3 us: reduce_hidden(): return lax.psum_scatter(total, 'y', scatter_dimension=0).astype(F32)]
    ppermute x1 -> x27, starting transfers between devices: 7.74 us -> 53.9 us  [the longest x12 29.5 us: move_section(): return lax.ppermute(array, ('section', 'z'), pairs)]
    all_gather x2 -> x6, waiting for transfers between devices: 125 us -> 88.1 us  [the longest x3 59.6 us: per_device(): same = lax.all_gather(block, 'y', axis=0)]
    pallas_call x0 -> x6, Pallas kernels: none -> 24.7 us  [the longest x3 13.3 us: feature_product(): pl.pallas_call(feature_kernel, grid=(width // tile,), in_specs=[pl.BlockS...]
    ppermute x1 -> x27, waiting for transfers between devices: 5.71 us -> 28.5 us  [the longest x12 14 us: move_section(): return lax.ppermute(array, ('section', 'z'), pairs)]
    unnamed x9 -> x39, local copies, waits for them, and re-layouts: 0.16 us -> 22.2 us
    dot_general x2 -> x0, matrix products: 20 us -> none  [contract_rows(): lax.dot_general(rows, weight_matrix, (((1,), (1,)), ((), ())), preferred_...]
  transfers between devices with their start and end apart: 5 -> 39, of which waited for: 5 -> 24; matrix products, arithmetic and copies ran while one was open for 0% -> 3% of each run, Pallas kernels for 0% -> 6%
where the time goes in v1:
time: 415 us; the launch traced here: 414 us
  waiting for transfers between devices  251 us (60%)
  starting transfers between devices  54.5 us (13%)
  local copies, waits for them, and re-layouts  32.4 us (8%)
  blocking collectives  27.4 us (7%)
  Pallas kernels  24.7 us (6%)
  between operations  14 us (3%)
  other arithmetic  10.4 us (3%)
    reduce_scatter x3, waiting for transfers between devices, reduce_hidden(): return lax.psum_scatter(total, 'y', scatter_dimension=0).astype(F32)  68.3 us
    reduce_scatter x3, waiting for transfers between devices, reduce_features(): total = lax.psum_scatter(parts, 'x', scatter_dimension=0)  64.1 us
    all_gather x3, waiting for transfers between devices, per_device(): same = lax.all_gather(block, 'y', axis=0)  59.6 us
    ppermute x12, starting transfers between devices, move_section(): return lax.ppermute(array, ('section', 'z'), pairs)  29.5 us
    all_gather x3, waiting for transfers between devices, gather_rows(): return lax.all_gather(own, 'x', axis=0)  28.6 us
    unnamed x39, local copies, waits for them, and re-layouts  22.2 us
    psum x1, blocking collectives, per_device(): lax.psum(jnp.stack([jnp.sum(scaled, axis=2), jnp.sum(scaled * entry, axis...  15.1 us
    ppermute x9, starting transfers between devices, move_z(): return lax.ppermute(array, 'z', [(z, z ^ flip) for z in range(4)])  14.3 us
  transfers between devices with their start and end apart: 39, of which 24 were waited for; matrix products, arithmetic and copies ran while one was open for 3% of the time, Pallas kernels for 6%

profile of v1, /device:TPU:1, one launch (start us, length us, event | category | flops | bytes accessed | tf_op | source)
XLA Modules:
  0.0 414.1 jit_solution(12236942783016698986)
XLA Ops:
  7.8 12.3 %all_to_all.13 = bf16[12,8,1024]{2,0,1:T(8,128)(2,1)S(1)} all-to-all(bf16[12,8,1024]{2,0,1:T(8,128)(2,1)S(1)} %copy.26), channel_id=1, replica_groups=mesh['section'=2,'y'=4,'core'=2,'z'=4,'x'=4] {'y','core'}, dimensions={1} | all-to-all | bytes 393216 | tf_op jit(solution)/shard_map/all_to_all | solution.py:174
  20.2 5.7 %collective-permute-start = (bf16[4,8,1024]{2,1,0:T(8,128)(2,1)S(1)}, bf16[4,8,1024]{2,1,0:T(8,128)(2,1)S(1)}, u32[]{:S(2)}, u32[]{:S(2)}) collective-permute-start(bf16[4,8,1024]{2,1,0:T(8,128)(2,1)S(1)} %copy.40), channel_id=1, source_target_pairs={{0,140},{4,136},{8,132},{12,128},{128,12},{132,8},{136,4},{140,0},... | collective-permute-start | bytes 196616 | tf_op jit(solution)/shard_map/ppermute | solution.py:22
  32.5 4.7 %collective-permute-done.3 = bf16[4,8,1024]{2,1,0:T(8,128)(2,1)S(1)} collective-permute-done((bf16[4,8,1024]{2,1,0:T(8,128)(2,1)S(1)}, bf16[4,8,1024]{2,1,0:T(8,128)(2,1)S(1)}, u32[]{:S(2)}, u32[]{:S(2)}) %collective-permute-start.3) | collective-permute-done | bytes 65568 | tf_op jit(solution)/shard_map/ppermute | solution.py:22
  39.7 4.8 %collective-permute-start.11 = (bf16[4,8,1024]{2,1,0:T(8,128)(2,1)S(1)}, bf16[4,8,1024]{2,1,0:T(8,128)(2,1)S(1)}, u32[]{:S(2)}, u32[]{:S(2)}) collective-permute-start(bf16[4,8,1024]{2,1,0:T(8,128)(2,1)S(1)} %copy.42), channel_id=1, source_target_pairs={{0,128},{4,132},{8,136},{12,140},{128,0},{132,4},{136,8},{140,12},... | collective-permute-start | bytes 196616 | tf_op jit(solution)/shard_map/ppermute | solution.py:22
  48.8 3.9 collective-permute-start.7
  60.4 3.9 collective-permute-done.8
  69.4 3.8 shard_map.73
  78.9 12.7 %all-gather.9.cloned.1.call-done.gathered = bf16[4,8,16,1024]{3,2,1,0:T(8,128)(2,1)} async-done(((bf16[1,8,16,1024]{3,2,1,0:T(8,128)(2,1)}), bf16[4,8,16,1024]{3,2,1,0:T(8,128)(2,1)}) %all-gather.9.cloned.1.call-update) | async-done | bytes 1048592 | tf_op jit(solution)/shard_map/all_gather | solution.py:144
  95.0 3.8 shard_map.74
  104.4 15.9 %all-gather.11.cloned.1.call-done.gathered = bf16[4,8,16,1024]{3,2,1,0:T(8,128)(2,1)} async-done(((bf16[1,8,16,1024]{3,2,1,0:T(8,128)(2,1)}), bf16[4,8,16,1024]{3,2,1,0:T(8,128)(2,1)}) %all-gather.11.cloned.1.call-update) | async-done | bytes 1048592 | tf_op jit(solution)/shard_map/all_gather | solution.py:144
  123.7 3.8 shard_map.75
  136.7 11.6 %reduce-scatter.7.cloned.1.call-done = bf16[1,64,2048]{2,1,0:T(8,128)(2,1)} async-done(((bf16[4,64,2048]{2,1,0:T(8,128)(2,1)}), bf16[1,64,2048]{2,1,0:T(8,128)(2,1)}) %reduce-scatter.7.cloned.1.call-update) | async-done | bytes 262160 | tf_op jit(solution)/shard_map/reduce_scatter | solution.py:149
  148.3 28.9 %reduce-scatter.11.cloned.1.call-done = bf16[1,64,2048]{2,1,0:T(8,128)(2,1)} async-done(((bf16[4,64,2048]{2,1,0:T(8,128)(2,1)}), bf16[1,64,2048]{2,1,0:T(8,128)(2,1)}) %reduce-scatter.11.cloned.1.call-update) | async-done | bytes 262160 | tf_op jit(solution)/shard_map/reduce_scatter | solution.py:149
  177.2 27.8 %reduce-scatter.15.cloned.1.call-done = bf16[1,64,2048]{2,1,0:T(8,128)(2,1)} async-done(((bf16[4,64,2048]{2,1,0:T(8,128)(2,1)}), bf16[1,64,2048]{2,1,0:T(8,128)(2,1)}) %reduce-scatter.15.cloned.1.call-update) | async-done | bytes 262160 | tf_op jit(solution)/shard_map/reduce_scatter | solution.py:149
  208.7 25.9 %all-gather.13.cloned.1.call-done.same = bf16[4,64,2048]{2,1,0:T(8,128)(2,1)} async-done(((bf16[1,64,2048]{2,1,0:T(8,128)(2,1)}), bf16[4,64,2048]{2,1,0:T(8,128)(2,1)}) %all-gather.13.cloned.1.call-update) | async-done | bytes 1048592 | tf_op jit(solution)/shard_map/all_gather | solution.py:196
  242.1 4.5 %shard_map.76 = bf16[4,4,32,1024]{3,2,1,0:T(8,128)(2,1)} custom-call(s32[4]{0:T(128)S(1)} %pad_add_fusion.pos, bf16[4,64,2048]{2,1,0:T(8,128)(2,1)S(1)} %copy-done.11, bf16[4,64,2048]{2,1,0:T(8,128)(2,1)S(1)} %collective-permute-done.13.other, bf16[1024,2048]{1,0:T(8,128)(2,1)S(1)} %bitcast.104), custom_call_target="tpu_custom_call" | custom-call | flops 2147483648 | bytes 7340032 | tf_op jit(solution)/shard_map/pallas_call | solution.py:111
  246.6 16.8 %all-gather.15.cloned.1.call-done.same = bf16[4,64,2048]{2,1,0:T(8,128)(2,1)} async-done(((bf16[1,64,2048]{2,1,0:T(8,128)(2,1)}), bf16[4,64,2048]{2,1,0:T(8,128)(2,1)}) %all-gather.15.cloned.1.call-update) | async-done | bytes 1048592 | tf_op jit(solution)/shard_map/all_gather | solution.py:196
  270.9 4.4 %shard_map.77 = bf16[4,4,32,1024]{3,2,1,0:T(8,128)(2,1)} custom-call(s32[4]{0:T(128)S(1)} %pad_add_fusion.pos, bf16[4,64,2048]{2,1,0:T(8,128)(2,1)S(1)} %copy-done.10, bf16[4,64,2048]{2,1,0:T(8,128)(2,1)S(1)} %collective-permute-done.18.other, bf16[1024,2048]{1,0:T(8,128)(2,1)S(1)} %bitcast.105), custom_call_target="tpu_custom_call" | custom-call | flops 2147483648 | bytes 7340032 | tf_op jit(solution)/shard_map/pallas_call | solution.py:111
  275.4 16.9 %all-gather.17.cloned.1.call-done.same = bf16[4,64,2048]{2,1,0:T(8,128)(2,1)} async-done(((bf16[1,64,2048]{2,1,0:T(8,128)(2,1)}), bf16[4,64,2048]{2,1,0:T(8,128)(2,1)}) %all-gather.17.cloned.1.call-update) | async-done | bytes 1048592 | tf_op jit(solution)/shard_map/all_gather | solution.py:196
  299.8 4.4 %shard_map.78 = bf16[4,4,32,1024]{3,2,1,0:T(8,128)(2,1)} custom-call(s32[4]{0:T(128)S(1)} %pad_add_fusion.pos, bf16[4,64,2048]{2,1,0:T(8,128)(2,1)S(1)} %copy-done.8, bf16[4,64,2048]{2,1,0:T(8,128)(2,1)S(1)} %collective-permute-done.23.other, bf16[1024,2048]{1,0:T(8,128)(2,1)S(1)} %bitcast.106), custom_call_target="tpu_custom_call" | custom-call | flops 2147483648 | bytes 7340032 | tf_op jit(solution)/shard_map/pallas_call | solution.py:111
  304.3 16.5 %reduce-scatter.9.cloned.1.call-done = bf16[1,4,32,1024]{3,2,1,0:T(8,128)(2,1)} async-done(((bf16[4,4,32,1024]{3,2,1,0:T(8,128)(2,1)}), bf16[1,4,32,1024]{3,2,1,0:T(8,128)(2,1)}) %reduce-scatter.9.cloned.1.call-update) | async-done | bytes 262160 | tf_op jit(solution)/shard_map/reduce_scatter | solution.py:153
  325.4 23.9 %reduce-scatter.13.cloned.1.call-done = bf16[1,4,32,1024]{3,2,1,0:T(8,128)(2,1)} async-done(((bf16[4,4,32,1024]{3,2,1,0:T(8,128)(2,1)}), bf16[1,4,32,1024]{3,2,1,0:T(8,128)(2,1)}) %reduce-scatter.13.cloned.1.call-update) | async-done | bytes 262160 | tf_op jit(solution)/shard_map/reduce_scatter | solution.py:153
  354.0 23.7 %reduce-scatter.17.cloned.1.call-done = bf16[1,4,32,1024]{3,2,1,0:T(8,128)(2,1)} async-done(((bf16[4,4,32,1024]{3,2,1,0:T(8,128)(2,1)}), bf16[1,4,32,1024]{3,2,1,0:T(8,128)(2,1)}) %reduce-scatter.17.cloned.1.call-update) | async-done | bytes 262160 | tf_op jit(solution)/shard_map/reduce_scatter | solution.py:153
  390.3 15.1 %psum.7 = f32[2,3,32]{2,1,0:T(4,128)S(1)} all-reduce(f32[2,3,32]{2,1,0:T(4,128)S(1)} %pad_maximum_fusion.3), channel_id=1, replica_groups=mesh['section'=2,'y'=4,'core'=2,'z'=4,'x'=4] {'y','core'}, use_global_device_ids=true, to_apply=%region_8.9 | all-reduce | flops 192 | bytes 1536 | tf_op jit(solution)/shard_map/psum | solution.py:202
  (161 shorter events, 104.4 us)
Async XLA Ops:
  6.5 59.4 %all-gather.7.cloned.1.call-start = ((), (), s32[]{:S(2)}) async-start(), calls=%async_computation.7 | async-start | bytes 1310720 | tf_op jit(solution)/shard_map/all_gather | solution.py:144
  20.2 11.5 %collective-permute-start = (bf16[4,8,1024]{2,1,0:T(8,128)(2,1)S(1)}, bf16[4,8,1024]{2,1,0:T(8,128)(2,1)S(1)}, u32[]{:S(2)}, u32[]{:S(2)}) collective-permute-start(bf16[4,8,1024]{2,1,0:T(8,128)(2,1)S(1)} %copy.40), channel_id=1, source_target_pairs={{0,140},{4,136},{8,132},{12,128},{128,12},{132,8},{136,4},{140,0},... | collective-permute-start | bytes 196616 | tf_op jit(solution)/shard_map/ppermute | solution.py:22
  38.2 53.4 %all-gather.9.cloned.1.call-start = ((), (), s32[]{:S(2)}) async-start(), calls=%async_computation.8 | async-start | bytes 1310720 | tf_op jit(solution)/shard_map/all_gather | solution.py:144
  39.7 13.0 %collective-permute-start.11 = (bf16[4,8,1024]{2,1,0:T(8,128)(2,1)S(1)}, bf16[4,8,1024]{2,1,0:T(8,128)(2,1)S(1)}, u32[]{:S(2)}, u32[]{:S(2)}) collective-permute-start(bf16[4,8,1024]{2,1,0:T(8,128)(2,1)S(1)} %copy.42), channel_id=1, source_target_pairs={{0,128},{4,132},{8,136},{12,140},{128,0},{132,4},{136,8},{140,12},... | collective-permute-start | bytes 196616 | tf_op jit(solution)/shard_map/ppermute | solution.py:22
  44.7 12.3 %collective-permute-start.5 = (bf16[4,8,1024]{2,1,0:T(8,128)(2,1)S(1)}, bf16[4,8,1024]{2,1,0:T(8,128)(2,1)S(1)}, u32[]{:S(2)}, u32[]{:S(2)}) collective-permute-start(bf16[4,8,1024]{2,1,0:T(8,128)(2,1)S(1)} %copy.41), channel_id=1, source_target_pairs={{0,136},{4,140},{8,128},{12,132},{128,8},{132,12},{136,0},{140,4},... | collective-permute-start | bytes 196616 | tf_op jit(solution)/shard_map/ppermute | solution.py:22
  47.4 13.0 %collective-permute-start.6 = (bf16[4,8,1024]{2,1,0:T(8,128)(2,1)S(1)}, bf16[4,8,1024]{2,1,0:T(8,128)(2,1)S(1)}, u32[]{:S(2)}, u32[]{:S(2)}) collective-permute-start(bf16[4,8,1024]{2,1,0:T(8,128)(2,1)S(1)} %copy.41), channel_id=1, source_target_pairs={{0,132},{4,128},{8,140},{12,136},{128,4},{132,0},{136,12},{140,8},... | collective-permute-start | bytes 196616 | tf_op jit(solution)/shard_map/ppermute | solution.py:22
  48.8 11.6 %collective-permute-start.7 = (bf16[4,8,1024]{2,1,0:T(8,128)(2,1)S(1)}, bf16[4,8,1024]{2,1,0:T(8,128)(2,1)S(1)}, u32[]{:S(2)}, u32[]{:S(2)}) collective-permute-start(bf16[4,8,1024]{2,1,0:T(8,128)(2,1)S(1)} %copy.41), channel_id=1, source_target_pairs={{0,128},{4,132},{8,136},{12,140},{128,0},{132,4},{136,8},{140,12},... | collective-permute-start | bytes 196616 | tf_op jit(solution)/shard_map/ppermute | solution.py:22
  52.7 11.6 %collective-permute-start.8 = (bf16[4,8,1024]{2,1,0:T(8,128)(2,1)S(1)}, bf16[4,8,1024]{2,1,0:T(8,128)(2,1)S(1)}, u32[]{:S(2)}, u32[]{:S(2)}) collective-permute-start(bf16[4,8,1024]{2,1,0:T(8,128)(2,1)S(1)} %copy.42), channel_id=1, source_target_pairs={{0,140},{4,136},{8,132},{12,128},{128,12},{132,8},{136,4},{140,0},... | collective-permute-start | bytes 196616 | tf_op jit(solution)/shard_map/ppermute | solution.py:22
  52.8 12.0 %collective-permute-start.9 = (bf16[4,8,1024]{2,1,0:T(8,128)(2,1)S(1)}, bf16[4,8,1024]{2,1,0:T(8,128)(2,1)S(1)}, u32[]{:S(2)}, u32[]{:S(2)}) collective-permute-start(bf16[4,8,1024]{2,1,0:T(8,128)(2,1)S(1)} %copy.42), channel_id=1, source_target_pairs={{0,136},{4,140},{8,128},{12,132},{128,8},{132,12},{136,0},{140,4},... | collective-permute-start | bytes 196616 | tf_op jit(solution)/shard_map/ppermute | solution.py:22
  65.8 54.5 %all-gather.11.cloned.1.call-start = ((), (), s32[]{:S(2)}) async-start(), calls=%async_computation.9 | async-start | bytes 1310720 | tf_op jit(solution)/shard_map/all_gather | solution.py:144
  76.1 72.2 %reduce-scatter.7.cloned.1.call-start = ((), (), s32[]{:S(2)}) async-start(), calls=%async_computation.10 | async-start | bytes 1310720 | tf_op jit(solution)/shard_map/reduce_scatter | solution.py:149
  78.8 98.4 %reduce-scatter.11.cloned.1.call-start = ((), (), s32[]{:S(2)}) async-start(), calls=%async_computation.13 | async-start | bytes 1310720 | tf_op jit(solution)/shard_map/reduce_scatter | solution.py:149
  104.2 100.8 %reduce-scatter.15.cloned.1.call-start = ((), (), s32[]{:S(2)}) async-start(), calls=%async_computation.16 | async-start | bytes 1310720 | tf_op jit(solution)/shard_map/reduce_scatter | solution.py:149
  132.9 101.7 %all-gather.13.cloned.1.call-start = ((), (), s32[]{:S(2)}) async-start(), calls=%async_computation.11 | async-start | bytes 1310720 | tf_op jit(solution)/shard_map/all_gather | solution.py:196
  207.2 56.3 %all-gather.15.cloned.1.call-start = ((), (), s32[]{:S(2)}) async-start(), calls=%async_computation.14 | async-start | bytes 1310720 | tf_op jit(solution)/shard_map/all_gather | solution.py:196
  207.9 84.4 %all-gather.17.cloned.1.call-start = ((), (), s32[]{:S(2)}) async-start(), calls=%async_computation.17 | async-start | bytes 1310720 | tf_op jit(solution)/shard_map/all_gather | solution.py:196
  208.7 112.1 %reduce-scatter.9.cloned.1.call-start = ((), (), s32[]{:S(2)}) async-start(), calls=%async_computation.12 | async-start | bytes 1310720 | tf_op jit(solution)/shard_map/reduce_scatter | solution.py:153
  246.5 102.7 %reduce-scatter.13.cloned.1.call-start = ((), (), s32[]{:S(2)}) async-start(), calls=%async_computation.15 | async-start | bytes 1310720 | tf_op jit(solution)/shard_map/reduce_scatter | solution.py:153
  275.4 102.3 %reduce-scatter.17.cloned.1.call-start = ((), (), s32[]{:S(2)}) async-start(), calls=%async_computation.18 | async-start | bytes 1310720 | tf_op jit(solution)/shard_map/reduce_scatter | solution.py:153
  321.7 56.9 %collective-permute-start.14 = (bf16[32,1024]{1,0:T(8,128)(2,1)S(1)}, bf16[32,1024]{1,0:T(8,128)(2,1)S(1)}, u32[]{:S(2)}, u32[]{:S(2)}) collective-permute-start(bf16[32,1024]{1,0:T(8,128)(2,1)S(1)} %get-tuple-element.43), channel_id=1, source_target_pairs={{0,4},{4,0},{8,12},{12,8},{1,5},{5,1},{9,13},{13,9},{2,6},{6,2},{1... | collective-permute-start | bytes 196616 | tf_op jit(solution)/shard_map/ppermute | solution.py:17
  323.1 58.8 %collective-permute-start.15 = (bf16[32,1024]{1,0:T(8,128)(2,1)S(1)}, bf16[32,1024]{1,0:T(8,128)(2,1)S(1)}, u32[]{:S(2)}, u32[]{:S(2)}) collective-permute-start(bf16[32,1024]{1,0:T(8,128)(2,1)S(1)} %get-tuple-element.45), channel_id=1, source_target_pairs={{0,8},{4,12},{8,0},{12,4},{1,9},{5,13},{9,1},{13,5},{2,10},{6,14},... | collective-permute-start | bytes 196616 | tf_op jit(solution)/shard_map/ppermute | solution.py:17
  325.3 56.6 %collective-permute-start.16 = (bf16[32,1024]{1,0:T(8,128)(2,1)S(1)}, bf16[32,1024]{1,0:T(8,128)(2,1)S(1)}, u32[]{:S(2)}, u32[]{:S(2)}) collective-permute-start(bf16[32,1024]{1,0:T(8,128)(2,1)S(1)} %get-tuple-element.44), channel_id=1, source_target_pairs={{0,12},{4,8},{8,4},{12,0},{1,13},{5,9},{9,5},{13,1},{2,14},{6,10},... | collective-permute-start | bytes 196616 | tf_op jit(solution)/shard_map/ppermute | solution.py:17
  350.2 32.1 %collective-permute-start.19 = (bf16[32,1024]{1,0:T(8,128)(2,1)S(1)}, bf16[32,1024]{1,0:T(8,128)(2,1)S(1)}, u32[]{:S(2)}, u32[]{:S(2)}) collective-permute-start(bf16[32,1024]{1,0:T(8,128)(2,1)S(1)} %get-tuple-element.36), channel_id=1, source_target_pairs={{0,4},{4,0},{8,12},{12,8},{1,5},{5,1},{9,13},{13,9},{2,6},{6,2},{1... | collective-permute-start | bytes 196616 | tf_op jit(solution)/shard_map/ppermute | solution.py:17
  351.7 35.4 %collective-permute-start.20 = (bf16[32,1024]{1,0:T(8,128)(2,1)S(1)}, bf16[32,1024]{1,0:T(8,128)(2,1)S(1)}, u32[]{:S(2)}, u32[]{:S(2)}) collective-permute-start(bf16[32,1024]{1,0:T(8,128)(2,1)S(1)} %get-tuple-element.38), channel_id=1, source_target_pairs={{0,8},{4,12},{8,0},{12,4},{1,9},{5,13},{9,1},{13,5},{2,10},{6,14},... | collective-permute-start | bytes 196616 | tf_op jit(solution)/shard_map/ppermute | solution.py:17
  (31 other events, 356.9 us)
Sparse Core Ops, SparseCore 0:
  38.3 24.5 all-gather.6
  65.9 25.6 all-gather.8
  93.4 26.8 all-gather.10
  122.7 25.5 reduce-scatter.6
  150.8 26.2 reduce-scatter.10
  179.6 25.3 reduce-scatter.14
  207.3 27.2 all-gather.12
  236.5 26.8 all-gather.14
  265.4 26.8 all-gather.16
  294.8 25.9 reduce-scatter.8
  323.4 25.8 reduce-scatter.12
  351.8 25.8 reduce-scatter.16
